TPU v7x, 256 devices: a whole 4x4x8 slice. The times are simulated.
256 devices in a mesh: ty: 8 (over x, z_lo), tx: 32 (over z_hi, y, core).
Axes of the slice: x: 4, y: 4, z: 8 (z_hi: 4, z_lo: 2; z = z_hi * 2 + z_lo), core: 2. Of those that a mesh axis runs over, the one named last changes fastest.
Arguments:
- mask_param: float32 [512, 4096], P('ty', 'tx'), may hold values from -12 to 12
- target: float32 [512, 4096], P('ty', 'tx'), may hold values from 0 to 1
- kernel_sets: bfloat16 [32, 8, 2, 128, 128], P('tx'), may hold values from -0.09375 to 0.09375
- kernel_weights: bfloat16 [32, 8], P('tx'), may hold values from 0.049804688 to 1
- tile_zones: int32 [8, 32, 2], P('ty', 'tx'), may hold values from 0 to 31
- tile_counts: int32 [8, 32], P('ty', 'tx'), may hold values from 1 to 2, as said below
- zone_to_set: int32 [32], replicated, may hold values from 0 to 31, each once
Outputs:
- resist: float32 [512, 4096], P('ty', 'tx')
- param_grad: float32 [512, 4096], P('ty', 'tx')
Inputs may be any that keep to these rules, and one draw needn't show every extreme that they name: `tile_zones`: zone ids; a tile uses only its first tile_counts slots. `tile_counts`: some tile has 2 live slots. `zone_to_set`: each kernel set belongs to exactly one zone.
All inputs are finite; a program needn't handle non-finite values.
Results may differ from a plain program's by a relative error of at most 0.00045.
Values may be sent and summed in bfloat16 or wider, within the bound.
A program may use at most 128 MiB of HBM per device.

v0:
```python
import functools

import jax
import jax.numpy as jnp
import ml_dtypes
import numpy as np
from jax import lax
from jax.experimental import pallas as pl
from jax.experimental.pallas import tpu as pltpu
from jax.sharding import PartitionSpec as P

BF = jnp.bfloat16
MESH = pl.DeviceIdType.MESH
XS, YC, ZH = 4, 8, 4
MEMBERS = XS * YC
TYS, TXS = 8, 32
AROUND = [(dr, dc) for dr in (-1, 0, 1) for dc in (-1, 0, 1) if (dr, dc) != (0, 0)]
E_ORDER = (4, 3, 5, 2, 6, 1, 7, 0)
DX_ORDER = (2, 1, 3, 0)


def tables():
    theta = np.pi * (2 * np.arange(128) + 1) / 256.0
    ky = 2 * np.pi / 192.0

    def split(a):
        hi = a.astype(ml_dtypes.bfloat16)
        lo = (a - hi.astype(np.float64)).astype(ml_dtypes.bfloat16)
        return hi, lo

    def left(a):
        hi, lo = split(a)
        return np.concatenate([hi, lo, hi], axis=1)

    def real_form(angle):
        c, s = np.cos(angle), np.sin(angle)
        return np.block([[c, -s], [s, c]])

    u, r, y = np.arange(192), np.arange(192), np.arange(64)
    ang = np.outer(np.arange(128), theta)
    hi, lo = split(np.concatenate([np.cos(ang), np.sin(ang)], axis=1))
    wk = np.concatenate([hi, lo], axis=0)
    a3 = left(real_form(ky * np.outer(u, np.arange(128))))
    b3 = left(real_form(ky * np.outer(y, u)))
    sc = 2.0 / (256 * 192)
    ang = np.outer(theta, np.arange(128))
    hi, lo = split(np.concatenate([np.cos(ang), -np.sin(ang)], axis=0) * sc)
    wi = np.concatenate([hi, lo], axis=1)
    ang = np.outer(np.arange(128), theta)
    hi, lo = split(np.concatenate([np.cos(ang), -np.sin(ang)], axis=1))
    wq = np.concatenate([hi, lo, hi], axis=0)
    aq3 = left(real_form(-ky * np.outer(u, y)))
    pos = np.arange(384) - 64
    live = ((pos >= 0) & (pos < 256)).astype(np.float64)
    ang = np.outer(pos, theta)
    hi, lo = split(np.concatenate([np.cos(ang), -np.sin(ang)], axis=1) * live[:, None])
    we = np.concatenate([hi, lo, hi], axis=0)
    ce3 = left(real_form(-ky * np.outer(u, r)))
    ct3 = left(real_form(ky * np.outer(r, u)))
    ang = np.outer(theta, pos)
    hi, lo = split(np.concatenate([np.cos(ang), -np.sin(ang)], axis=0) * sc * live[None, :])
    wt = np.concatenate([hi, lo, hi], axis=0)
    return dict(wk=wk, a3=a3, b3=b3, wi=wi, wq=wq, aq3=aq3, we=we, ce3=ce3, ct3=ct3, wt=wt)

NAMES = ("wk", "a3", "b3", "wi", "wq", "aq3", "we", "ce3", "ct3", "wt")

def hilo(a):
    hi = a.astype(BF)
    return hi, (a - hi.astype(jnp.float32)).astype(BF)

def dot(a, b):
    return jnp.dot(a, b, preferred_element_type=jnp.float32)

def rows3(a):
    hi, lo = hilo(a)
    return jnp.concatenate([hi, hi, lo], axis=0)

def cols3(a):
    hi, lo = hilo(a)
    return jnp.concatenate([hi, hi, lo], axis=1)

def swap(a):
    m, n = a.shape[0] // 2, a.shape[1] // 2
    top = jnp.concatenate([a[:m, :n], a[m:, :n]], axis=1)
    low = jnp.concatenate([a[:m, n:], a[m:, n:]], axis=1)
    return jnp.concatenate([top, low], axis=0)

def mask_spectrum(e9, we, ce3, e2):
    packed = dot(cols3(e9), we)
    tall = jnp.concatenate([packed[:, :128], packed[:, 128:]], axis=0)
    spec = dot(ce3, rows3(tall))
    e2[:, :128] = spec
    e2[:, 128:] = spec

def kernel_spectrum(tr, ti, t, k2, p):
    both = jnp.concatenate([tr, ti], axis=0)
    packed = dot(jnp.concatenate([both, both], axis=1), t["wk"][...])
    k2[p] = dot(t["a3"][...], rows3(swap(packed)))

def field(t, e2, k2, f, p):
    er, ei = e2[:192, :], e2[192:, :]
    kr, ki = k2[p, :192, :], k2[p, 192:, :]
    prod = jnp.concatenate([er * kr - ei * ki, er * ki + ei * kr], axis=0)
    z = swap(dot(t["b3"][...], rows3(prod)))
    hi, lo = hilo(z)
    first = dot(hi, t["wi"][...])
    out = first[:, :128] + first[:, 128:] + dot(lo, t["wi"][:, :128])
    f[p] = out
    return out

def spread(t, k2, q, p, tr, ti):
    packed = dot(cols3(q), t["wq"][...])
    q2 = dot(t["aq3"][...], rows3(swap(packed)))
    qr, qi = q2[:192], q2[192:]
    kr, ki = k2[p, :192, :], k2[p, 192:, :]
    tr[...] += qr * kr + qi * ki
    ti[...] += qi * kr - qr * ki

def back(t, tr, ti):
    total = jnp.concatenate([tr[:, :128] + tr[:, 128:], ti[:, :128] + ti[:, 128:]], axis=0)
    y = dot(t["ct3"][...], rows3(total))
    wide = jnp.concatenate([y[:192], y[192:]], axis=1)
    return dot(cols3(wide), t["wt"][...])

def slot_of(dr, dc):
    return (dr + 1) * 3 + dc + 1


def kernel(*refs):
    (mask_in, target_in, sets, wts, zones, counts, zone_to_set) = refs[:7]
    hbm = dict(zip(NAMES, refs[7:17]))
    resist_out, grad_out = refs[17:19]
    t = dict(zip(NAMES, refs[19:29]))
    (mask, target, value, tiles, chunks, info, sel, taps, wall, sv, wv, e2, k2, f, tr, ti, co, g9, gin,
     tab_sem, in_sem, own_sem, zsem, s_info, r_info, s_info2, r_info2, s_w, r_w, s_w2, r_w2,
     s1, r1, s2, r2, s_m, r_m, s_g, r_g) = refs[29:]

    ty, tx = lax.axis_index("ty"), lax.axis_index("tx")
    x, zl = ty // 2, ty % 2
    zh, yc = tx // YC, tx % YC
    me = x * YC + yc

    def remote(src, dst, send, recv, to):
        return pltpu.make_async_remote_copy(src, dst, send, recv, device_id=to, device_id_type=MESH)

    def done(ref, sem):
        pltpu.make_async_copy(ref, ref, sem).wait()

    copies_in = [pltpu.make_async_copy(mask_in, mask, in_sem.at[0]),
                 pltpu.make_async_copy(target_in, target, in_sem.at[1])]
    for c in copies_in:
        c.start()
    own = pltpu.make_async_copy(sets.at[me], chunks.at[tx], own_sem.at[0])
    own.start()
    tabs = [pltpu.make_async_copy(hbm[n], t[n], tab_sem.at[i]) for i, n in enumerate(NAMES)]
    for c in tabs:
        c.start()

    yc_line = [(yc + e) % YC for e in E_ORDER[:-1]]
    x_line = [(x + dx) % XS for dx in DX_ORDER[:-1]]
    up = 2 * zl + ZH - 1

    def z_target(m):
        if m == 3:
            return x * 2 + (1 - zl), (zh + 2) % ZH
        return x * 2 + (m - 1), (zh + up) % ZH

    z_sources = [(x * 2 + 1, (zh + ZH - 1) % ZH), (x * 2, (zh + 1) % ZH), (x * 2 + (1 - zl), (zh + 2) % ZH)]
    z_both = [(ty, (zh + ZH - 1) % ZH), (ty, (zh + 1) % ZH),
              (x * 2 + (1 - zl), (zh + up) % ZH), (x * 2 + (1 - zl), (zh + 2) % ZH)]

    def beside(dr, dc):
        return (ty + dr + TYS) % TYS, (tx + dc + TXS) % TXS

    bar = pltpu.get_barrier_semaphore()
    greet = [(a, b * YC + yc) for a, b in z_both]
    greet += [(a * 2 + zl, tx) for a in x_line]
    greet += [(ty, zh * YC + b) for b in yc_line]
    greet += [beside(dr, dc) for dr, dc in AROUND]
    for to in greet:
        pl.semaphore_signal(bar, 1, device_id=to, device_id_type=MESH)

    lane = lax.broadcasted_iota(jnp.int32, (1, 128), 1)
    my0, my1 = zone_to_set[zones[0]], zone_to_set[zones[1]]
    count = counts[0]
    sv[...] = jnp.where(lane == 0, my0, my1)
    wv[...] = jnp.concatenate([wts[...].astype(jnp.float32), jnp.zeros((1, 120), jnp.float32)], axis=1)
    for c in copies_in:
        c.wait()
    value[...] = 1.0 / (1.0 + jnp.exp(-mask[...]))

    pl.semaphore_wait(bar, len(greet))

    for i, a in enumerate(x_line):
        remote(sv, info.at[yc, x], s_info.at[i], r_info.at[i], (a * 2 + zl, tx)).start()
    for i, (a, b) in enumerate(z_sources):
        pl.semaphore_signal(zsem, 1, device_id=(a, b * YC + yc), device_id_type=MESH)
    for m in (3, 2, 1):
        a, b = z_target(m)
        remote(wv, wall.at[yc, zh], s_w, r_w, (a, b * YC + yc)).start()
    for m in (3, 2, 1):
        a, b = z_target(m)
        remote(sets.at[me], chunks.at[tx], s1, r1, (a, b * YC + yc)).start()
    for b in yc_line:
        remote(sets.at[x * YC + b], chunks.at[tx], s1, r1, (ty, zh * YC + b)).start()
    info[yc, x] = sv[...]
    wall[yc, zh] = wv[...]
    for i in range(3):
        done(info.at[0, 0], r_info.at[i])
    pl.semaphore_wait(zsem, 3)
    for m in (3, 2, 1):
        a, b = z_target(m)
        for y2 in yc_line:
            remote(sets.at[x * YC + y2], chunks.at[tx], s1, r1, (a, b * YC + y2)).start()
    for b in yc_line:
        remote(info.at[yc], info.at[yc], s_info2, r_info2, (ty, zh * YC + b)).start()
    done(wall.at[0, pl.ds(0, 3)], r_w)
    for b in yc_line:
        remote(wall.at[yc], wall.at[yc], s_w2, r_w2, (ty, zh * YC + b)).start()
    for dr, dc in AROUND:
        remote(value, tiles.at[slot_of(-dr, -dc)], s_m, r_m, beside(dr, dc)).start()
    tiles[slot_of(0, 0)] = value[...]
    for c in tabs:
        c.wait()
    done(tiles.at[pl.ds(0, 8)], r_m)

    def tile_at(dr, dc):
        block = tiles[slot_of(dr, dc)]
        if (dr, dc) == (0, 0):
            return block
        row, col = ty + dr, tx + dc
        inside = (row >= 0) & (row < TYS) & (col >= 0) & (col < TXS)
        return jnp.where(inside, block, 0.0)

    e9 = jnp.concatenate([jnp.concatenate([tile_at(dr, dc) for dc in (-1, 0, 1)], axis=1) for dr in (-1, 0, 1)], axis=0)
    mask_spectrum(e9, t["we"][...], t["ce3"][...], e2)
    own.wait()
    done(info.at[pl.ds(0, 7)], r_info2)
    done(chunks.at[pl.ds(0, 31)], r1)

    def select(i, s0, s1_):
        sel[i, 0] = chunks[s0]
        sel[i, 1] = chunks[s1_]

    for dx in DX_ORDER:
        for e in E_ORDER:
            if (dx, e) == (0, 0):
                continue
            x2, y2 = (x + dx) % XS, (yc + e) % YC
            row = info[y2, x2]
            i = dx * YC + e
            select(i, row[0, 0], row[0, 1])
            remote(sel.at[i], taps.at[me], s2, r2.at[dx], (x2 * 2 + zl, zh * YC + y2)).start()
    select(0, my0, my1)
    local = pltpu.make_async_copy(sel.at[0], taps.at[me], r2.at[0])
    local.start()

    for i in range(3):
        done(sv, s_info.at[i])
    done(wall.at[0, pl.ds(0, 3)], s_w)
    done(wall.at[pl.ds(0, 7)], r_w2)
    done(wall.at[pl.ds(0, 7)], s_w2)
    done(info.at[pl.ds(0, 7)], s_info2)
    done(tiles.at[pl.ds(0, 8)], s_m)
    done(chunks.at[pl.ds(0, 31)], s1)

    inverse = 1.0 / count.astype(jnp.float32)
    for j, s in enumerate((my0, my1)):
        row = wall[s % YC, s // YC]
        row = row * jnp.where(j < count, inverse, 0.0)
        for k in range(8):
            co[j * 8 + k] = jnp.broadcast_to(row[:, k:k + 1], (64, 128))

    aerial = jnp.zeros((64, 128), jnp.float32)
    for dx in DX_ORDER:
        done(taps.at[pl.ds(0, 8)], r2.at[dx])
        xs = (x + XS - dx) % XS

        def some(i, total):
            j, k = i // 2, 2 * xs + i % 2
            p = j * 8 + k
            first = jnp.concatenate([taps[4 * k, j], taps[4 * k + 1, j]], axis=0)
            second = jnp.concatenate([taps[4 * k + 2, j], taps[4 * k + 3, j]], axis=0)
            kernel_spectrum(first, second, t, k2, p)
            fp = field(t, e2, k2, f, p)
            return total + co[p] * (fp[:64] * fp[:64] + fp[64:] * fp[64:])

        aerial = lax.fori_loop(0, 4, some, aerial, unroll=2)

    done(sel.at[pl.ds(0, 31)], s2)
    resist = 1.0 / (1.0 + jnp.exp(-8.0 * (aerial - 1.0)))
    resist_out[...] = resist
    slope = 2.0 * (16.0 * (resist - target[...]) * 8.0 * resist * (1.0 - resist))
    tr[...] = jnp.zeros(tr.shape, jnp.float32)
    ti[...] = jnp.zeros(ti.shape, jnp.float32)

    def three(p, carry):
        g = slope * co[p]
        spread(t, k2, jnp.concatenate([g, g], axis=0) * f[p], p, tr, ti)
        return carry

    lax.fori_loop(0, 16, three, 0, unroll=2)
    g9[...] = back(t, tr, ti)
    for dr, dc in AROUND:
        src = g9.at[pl.ds((dr + 1) * 64, 64), pl.ds((dc + 1) * 128, 128)]
        remote(src, gin.at[slot_of(-dr, -dc)], s_g, r_g, beside(dr, dc)).start()
    gin[slot_of(0, 0)] = g9[64:128, 128:256]
    done(gin.at[pl.ds(0, 8)], r_g)
    total = gin[slot_of(0, 0)]
    for dr, dc in AROUND:
        row, col = ty + dr, tx + dc
        inside = (row >= 0) & (row < TYS) & (col >= 0) & (col < TXS)
        total = total + jnp.where(inside, gin[slot_of(dr, dc)], 0.0)
    m = value[...]
    grad_out[...] = total * m * (1.0 - m)
    done(gin.at[pl.ds(0, 8)], s_g)


def body(mask_param, target, kernel_sets, kernel_weights, tile_zones, tile_counts, zone_to_set):
    tb = tables()
    f32, i32, dma = jnp.float32, jnp.int32, pltpu.SemaphoreType.DMA
    any_, vmem = pl.BlockSpec(memory_space=pltpu.HBM), pl.BlockSpec(memory_space=pltpu.VMEM)
    smem = pl.BlockSpec(memory_space=pltpu.SMEM)
    scratch = [pltpu.VMEM(tb[n].shape, BF) for n in NAMES]
    scratch += [
        pltpu.VMEM((64, 128), f32), pltpu.VMEM((64, 128), f32), pltpu.VMEM((64, 128), f32),
        pltpu.VMEM((9, 64, 128), f32),
        pltpu.VMEM((32, 64, 128), BF), pltpu.VMEM((YC, XS, 1, 128), i32),
        pltpu.VMEM((32, 2, 64, 128), BF), pltpu.VMEM((32, 2, 64, 128), BF),
        pltpu.VMEM((YC, ZH, 1, 128), f32), pltpu.VMEM((1, 128), i32), pltpu.VMEM((1, 128), f32),
        pltpu.VMEM((384, 256), f32), pltpu.VMEM((16, 384, 256), f32), pltpu.VMEM((16, 128, 128), f32),
        pltpu.VMEM((192, 256), f32), pltpu.VMEM((192, 256), f32), pltpu.VMEM((16, 64, 128), f32),
        pltpu.VMEM((192, 384), f32), pltpu.VMEM((9, 64, 128), f32),
        dma((len(NAMES),)), dma((2,)), dma((1,)), pltpu.SemaphoreType.REGULAR,
        dma((3,)), dma((3,)), dma, dma, dma, dma, dma, dma,
        dma, dma, dma, dma((4,)), dma, dma, dma, dma,
    ]
    return pl.pallas_call(
        kernel,
        out_shape=(jax.ShapeDtypeStruct((64, 128), f32), jax.ShapeDtypeStruct((64, 128), f32)),
        in_specs=[any_, any_, any_, vmem, smem, smem, smem] + [any_] * len(NAMES),
        out_specs=(vmem, vmem),
        scratch_shapes=scratch,
        compiler_params=pltpu.CompilerParams(
            collective_id=1, has_side_effects=True, vmem_limit_bytes=63 << 20
        ),
        name="litho",
    )(
        mask_param, target, kernel_sets.reshape(32, 64, 128), kernel_weights,
        tile_zones.reshape(2), tile_counts.reshape(1), zone_to_set,
        *[jnp.asarray(tb[n]) for n in NAMES],
    )


def solution(mesh):
    in_specs = (
        P("ty", "tx"), P("ty", "tx"), P("tx", None, None, None, None), P("tx", None),
        P("ty", "tx", None), P("ty", "tx"), P(),
    )
    return jax.shard_map(
        body, mesh=mesh, in_specs=in_specs, out_specs=(P("ty", "tx"), P("ty", "tx")), check_vma=False
    )
```

profile of v0, /device:TPU:32, one launch (start us, length us, event | category | flops | bytes accessed | tf_op | source)
XLA Modules:
  0.0 73.9 jit_solution(7878373323272418352)
XLA Ops:
  1.3 70.6 %litho.1 = (f32[64,128]{1,0:T(8,128)}, f32[64,128]{1,0:T(8,128)}) custom-call(f32[64,128]{1,0:T(8,128)} %refs_0_.1, f32[64,128]{1,0:T(8,128)} %refs_1_.1, bf16[32,64,128]{2,1,0:T(8,128)(2,1)} %bitcast.4, bf16[1,8]{1,0:T(2,128)(2,1)} %refs_3_.1, s32[2]{0:T(128)} %bitcast.5, s32[1]{0:T(128)} %bitcast.3.refs_5_, s32[32]{0:T(128)} %refs_6_.1, ...), custom_call_target="tpu_custom_call" | custom-call | tf_op jit(solution)/shard_map/litho/pallas_call | solution.py:338
  71.9 0.0 copy-start
  71.9 1.4 %copy.22 = f32[64,128]{1,0:T(8,128)} copy(f32[64,128]{1,0:T(8,128)} %get-tuple-element.4) | data formatting | bytes 65536
  73.3 0.0 copy-done
  73.3 0.6 copy.23
Async XLA Ops:
  71.9 1.4 %copy-start = (f32[64,128]{1,0:T(8,128)S(1)}, f32[64,128]{1,0:T(8,128)}, u32[]{:S(2)}) copy-start(f32[64,128]{1,0:T(8,128)} %get-tuple-element.5) | copy-start | bytes 98308
where the time goes:
time: 74.1 us; the launch traced here: 73.9 us
  Pallas kernels  70.6 us (95%)
  local copies, waits for them, and re-layouts  2 us (3%)
  between operations  1.29 us (2%)
    pallas_call x1, Pallas kernels, body(): pl.pallas_call(kernel, out_shape=(jax.ShapeDtypeStruct((64, 128), f32), j...  70.6 us
    unnamed x4, local copies, waits for them, and re-layouts  2 us

commit v1 on v0

--- a/solution.py
+++ b/solution.py
@@ -17,6 +17,7 @@
 AROUND = [(dr, dc) for dr in (-1, 0, 1) for dc in (-1, 0, 1) if (dr, dc) != (0, 0)]
 E_ORDER = (4, 3, 5, 2, 6, 1, 7, 0)
 DX_ORDER = (2, 1, 3, 0)
+TY_ORDER = [(dx, dz) for dx in DX_ORDER for dz in (1, 0)]
 
 
 def tables():
@@ -138,7 +139,7 @@
     ty, tx = lax.axis_index("ty"), lax.axis_index("tx")
     x, zl = ty // 2, ty % 2
     zh, yc = tx // YC, tx % YC
-    me = x * YC + yc
+    me = ty * YC + yc
 
     def remote(src, dst, send, recv, to):
         return pltpu.make_async_remote_copy(src, dst, send, recv, device_id=to, device_id_type=MESH)
@@ -157,7 +158,7 @@
         c.start()
 
     yc_line = [(yc + e) % YC for e in E_ORDER[:-1]]
-    x_line = [(x + dx) % XS for dx in DX_ORDER[:-1]]
+    ty_line = [((x + dx) % XS) * 2 + (zl + dz) % 2 for dx, dz in TY_ORDER[:-1]]
     up = 2 * zl + ZH - 1
 
     def z_target(m):
@@ -174,7 +175,7 @@
 
     bar = pltpu.get_barrier_semaphore()
     greet = [(a, b * YC + yc) for a, b in z_both]
-    greet += [(a * 2 + zl, tx) for a in x_line]
+    greet += [(a, tx) for a in ty_line]
     greet += [(ty, zh * YC + b) for b in yc_line]
     greet += [beside(dr, dc) for dr, dc in AROUND]
     for to in greet:
@@ -191,8 +192,8 @@
 
     pl.semaphore_wait(bar, len(greet))
 
-    for i, a in enumerate(x_line):
-        remote(sv, info.at[yc, x], s_info.at[i], r_info.at[i], (a * 2 + zl, tx)).start()
+    for a in ty_line:
+        remote(sv, info.at[yc, ty], s_info, r_info, (a, tx)).start()
     for i, (a, b) in enumerate(z_sources):
         pl.semaphore_signal(zsem, 1, device_id=(a, b * YC + yc), device_id_type=MESH)
     for m in (3, 2, 1):
@@ -200,18 +201,17 @@
         remote(wv, wall.at[yc, zh], s_w, r_w, (a, b * YC + yc)).start()
     for m in (3, 2, 1):
         a, b = z_target(m)
-        remote(sets.at[me], chunks.at[tx], s1, r1, (a, b * YC + yc)).start()
+        remote(sets.at[a * YC + yc], chunks.at[tx], s1, r1, (a, b * YC + yc)).start()
     for b in yc_line:
-        remote(sets.at[x * YC + b], chunks.at[tx], s1, r1, (ty, zh * YC + b)).start()
-    info[yc, x] = sv[...]
+        remote(sets.at[ty * YC + b], chunks.at[tx], s1, r1, (ty, zh * YC + b)).start()
+    info[yc, ty] = sv[...]
     wall[yc, zh] = wv[...]
-    for i in range(3):
-        done(info.at[0, 0], r_info.at[i])
+    done(info.at[0, pl.ds(0, 7)], r_info)
     pl.semaphore_wait(zsem, 3)
     for m in (3, 2, 1):
         a, b = z_target(m)
         for y2 in yc_line:
-            remote(sets.at[x * YC + y2], chunks.at[tx], s1, r1, (a, b * YC + y2)).start()
+            remote(sets.at[a * YC + y2], chunks.at[tx], s1, r1, (a, b * YC + y2)).start()
     for b in yc_line:
         remote(info.at[yc], info.at[yc], s_info2, r_info2, (ty, zh * YC + b)).start()
     done(wall.at[0, pl.ds(0, 3)], r_w)
@@ -220,6 +220,28 @@
     for dr, dc in AROUND:
         remote(value, tiles.at[slot_of(-dr, -dc)], s_m, r_m, beside(dr, dc)).start()
     tiles[slot_of(0, 0)] = value[...]
+    own.wait()
+    done(info.at[pl.ds(0, 7)], r_info2)
+    done(chunks.at[pl.ds(0, 31)], r1)
+
+
+    def send_slot(j):
+        for n, (dx, dz) in enumerate(TY_ORDER):
+            ty2 = ((x + dx) % XS) * 2 + (zl + dz) % 2
+            for e in E_ORDER:
+                if (dx, dz, e) == (0, 0, 0):
+                    continue
+                y2 = (yc + e) % YC
+                i = n * YC + e
+                sel[j, i] = chunks[info[y2, ty2][0, j]]
+                remote(sel.at[j, i], taps.at[j, me], s2.at[j], r2.at[j], (ty2, zh * YC + y2)).start()
+        sel[j, 56] = chunks[(my0, my1)[j]]
+        pltpu.make_async_copy(sel.at[j, 56], taps.at[j, me], r2.at[j]).start()
+
+    send_slot(0)
+    done(sel.at[0, pl.ds(0, 63)], s2.at[0])
+    send_slot(1)
+
     for c in tabs:
         c.wait()
     done(tiles.at[pl.ds(0, 8)], r_m)
@@ -234,29 +256,7 @@
 
     e9 = jnp.concatenate([jnp.concatenate([tile_at(dr, dc) for dc in (-1, 0, 1)], axis=1) for dr in (-1, 0, 1)], axis=0)
     mask_spectrum(e9, t["we"][...], t["ce3"][...], e2)
-    own.wait()
-    done(info.at[pl.ds(0, 7)], r_info2)
-    done(chunks.at[pl.ds(0, 31)], r1)
-
-    def select(i, s0, s1_):
-        sel[i, 0] = chunks[s0]
-        sel[i, 1] = chunks[s1_]
-
-    for dx in DX_ORDER:
-        for e in E_ORDER:
-            if (dx, e) == (0, 0):
-                continue
-            x2, y2 = (x + dx) % XS, (yc + e) % YC
-            row = info[y2, x2]
-            i = dx * YC + e
-            select(i, row[0, 0], row[0, 1])
-            remote(sel.at[i], taps.at[me], s2, r2.at[dx], (x2 * 2 + zl, zh * YC + y2)).start()
-    select(0, my0, my1)
-    local = pltpu.make_async_copy(sel.at[0], taps.at[me], r2.at[0])
-    local.start()
-
-    for i in range(3):
-        done(sv, s_info.at[i])
+    done(info.at[0, pl.ds(0, 7)], s_info)
     done(wall.at[0, pl.ds(0, 3)], s_w)
     done(wall.at[pl.ds(0, 7)], r_w2)
     done(wall.at[pl.ds(0, 7)], s_w2)
@@ -272,22 +272,23 @@
             co[j * 8 + k] = jnp.broadcast_to(row[:, k:k + 1], (64, 128))
 
     aerial = jnp.zeros((64, 128), jnp.float32)
-    for dx in DX_ORDER:
-        done(taps.at[pl.ds(0, 8)], r2.at[dx])
-        xs = (x + XS - dx) % XS
-
-        def some(i, total):
-            j, k = i // 2, 2 * xs + i % 2
+    for j in range(2):
+        done(taps.at[j], r2.at[j])
+
+        def spectra(k, carry):
+            first, second = [taps[j, pl.ds(8 * k + 4 * i, 4)].reshape(128, 128) for i in range(2)]
+            kernel_spectrum(first, second, t, k2, j * 8 + k)
+            return carry
+
+        def fields(k, total):
             p = j * 8 + k
-            first = jnp.concatenate([taps[4 * k, j], taps[4 * k + 1, j]], axis=0)
-            second = jnp.concatenate([taps[4 * k + 2, j], taps[4 * k + 3, j]], axis=0)
-            kernel_spectrum(first, second, t, k2, p)
             fp = field(t, e2, k2, f, p)
             return total + co[p] * (fp[:64] * fp[:64] + fp[64:] * fp[64:])
 
-        aerial = lax.fori_loop(0, 4, some, aerial, unroll=2)
-
-    done(sel.at[pl.ds(0, 31)], s2)
+        lax.fori_loop(0, 8, spectra, 0, unroll=8)
+        aerial = lax.fori_loop(0, 8, fields, aerial, unroll=8)
+
+    done(sel.at[1, pl.ds(0, 63)], s2.at[1])
     resist = 1.0 / (1.0 + jnp.exp(-8.0 * (aerial - 1.0)))
     resist_out[...] = resist
     slope = 2.0 * (16.0 * (resist - target[...]) * 8.0 * resist * (1.0 - resist))
@@ -299,7 +300,7 @@
         spread(t, k2, jnp.concatenate([g, g], axis=0) * f[p], p, tr, ti)
         return carry
 
-    lax.fori_loop(0, 16, three, 0, unroll=2)
+    lax.fori_loop(0, 16, three, 0, unroll=8)
     g9[...] = back(t, tr, ti)
     for dr, dc in AROUND:
         src = g9.at[pl.ds((dr + 1) * 64, 64), pl.ds((dc + 1) * 128, 128)]
@@ -325,15 +326,15 @@
     scratch += [
         pltpu.VMEM((64, 128), f32), pltpu.VMEM((64, 128), f32), pltpu.VMEM((64, 128), f32),
         pltpu.VMEM((9, 64, 128), f32),
-        pltpu.VMEM((32, 64, 128), BF), pltpu.VMEM((YC, XS, 1, 128), i32),
-        pltpu.VMEM((32, 2, 64, 128), BF), pltpu.VMEM((32, 2, 64, 128), BF),
+        pltpu.VMEM((32, 32, 128), BF), pltpu.VMEM((YC, TYS, 1, 128), i32),
+        pltpu.VMEM((2, 64, 32, 128), BF), pltpu.VMEM((2, 64, 32, 128), BF),
         pltpu.VMEM((YC, ZH, 1, 128), f32), pltpu.VMEM((1, 128), i32), pltpu.VMEM((1, 128), f32),
         pltpu.VMEM((384, 256), f32), pltpu.VMEM((16, 384, 256), f32), pltpu.VMEM((16, 128, 128), f32),
         pltpu.VMEM((192, 256), f32), pltpu.VMEM((192, 256), f32), pltpu.VMEM((16, 64, 128), f32),
         pltpu.VMEM((192, 384), f32), pltpu.VMEM((9, 64, 128), f32),
         dma((len(NAMES),)), dma((2,)), dma((1,)), pltpu.SemaphoreType.REGULAR,
-        dma((3,)), dma((3,)), dma, dma, dma, dma, dma, dma,
-        dma, dma, dma, dma((4,)), dma, dma, dma, dma,
+        dma, dma, dma, dma, dma, dma, dma, dma,
+        dma, dma, dma((2,)), dma((2,)), dma, dma, dma, dma,
     ]
     return pl.pallas_call(
         kernel,
@@ -346,7 +347,7 @@
         ),
         name="litho",
     )(
-        mask_param, target, kernel_sets.reshape(32, 64, 128), kernel_weights,
+        mask_param, target, kernel_sets.reshape(64, 32, 128), kernel_weights,
         tile_zones.reshape(2), tile_counts.reshape(1), zone_to_set,
         *[jnp.asarray(tb[n]) for n in NAMES],
     )

time: 74.1 us -> 63.9 us (0.86)
  Pallas kernels: 70.6 us -> 60.5 us
    pallas_call x1, Pallas kernels: 70.6 us -> 60.5 us  [body(): pl.pallas_call(kernel, out_shape=(jax.ShapeDtypeStruct((64, 128), f32), j...]
where the time goes in v1:
time: 63.9 us; the launch traced here: 63.8 us
  Pallas kernels  60.5 us (95%)
  local copies, waits for them, and re-layouts  2 us (3%)
  between operations  1.29 us (2%)
    pallas_call x1, Pallas kernels, body(): pl.pallas_call(kernel, out_shape=(jax.ShapeDtypeStruct((64, 128), f32), j...  60.5 us
    unnamed x4, local copies, waits for them, and re-layouts  2 us

profile of v1, /device:TPU:32, one launch (start us, length us, event | category | flops | bytes accessed | tf_op | source)
XLA Modules:
  0.0 63.8 jit_solution(13391683740665620281)
XLA Ops:
  1.3 60.5 %litho.1 = (f32[64,128]{1,0:T(8,128)}, f32[64,128]{1,0:T(8,128)}) custom-call(f32[64,128]{1,0:T(8,128)} %refs_0_.1, f32[64,128]{1,0:T(8,128)} %refs_1_.1, bf16[64,32,128]{2,1,0:T(8,128)(2,1)} %bitcast.4, bf16[1,8]{1,0:T(2,128)(2,1)} %refs_3_.1, s32[2]{0:T(128)} %bitcast.5, s32[1]{0:T(128)} %bitcast.3.refs_5_, s32[32]{0:T(128)} %refs_6_.1, ...), custom_call_target="tpu_custom_call" | custom-call | tf_op jit(solution)/shard_map/litho/pallas_call | solution.py:339
  61.8 0.0 copy-start
  61.8 1.4 %copy.22 = f32[64,128]{1,0:T(8,128)} copy(f32[64,128]{1,0:T(8,128)} %get-tuple-element.4) | data formatting | bytes 65536
  63.2 0.0 copy-done
  63.2 0.6 copy.23
Async XLA Ops:
  61.8 1.4 %copy-start = (f32[64,128]{1,0:T(8,128)S(1)}, f32[64,128]{1,0:T(8,128)}, u32[]{:S(2)}) copy-start(f32[64,128]{1,0:T(8,128)} %get-tuple-element.5) | copy-start | bytes 98308

commit v2 on v1

v2 whole, which is shorter than its diff:
```python
import functools

import jax
import jax.numpy as jnp
import ml_dtypes
import numpy as np
from jax import lax
from jax.experimental import pallas as pl
from jax.experimental.pallas import tpu as pltpu
from jax.sharding import PartitionSpec as P

BF = jnp.bfloat16
MESH = pl.DeviceIdType.MESH
XS, YC, ZH = 4, 8, 4
MEMBERS = XS * YC
TYS, TXS = 8, 32
AROUND = [(dr, dc) for dr in (-1, 0, 1) for dc in (-1, 0, 1) if (dr, dc) != (0, 0)]
E_ORDER = (4, 3, 5, 2, 6, 1, 7, 0)
DX_ORDER = (2, 1, 3, 0)
TY_ORDER = [(dx, dz) for dx in DX_ORDER for dz in (1, 0)]


def tables():
    alpha = 2 * np.pi * (np.arange(96) + 0.5) / 192
    beta = 2 * np.pi * (np.arange(128) + 0.5) / 256
    scale = 2.0 / (192 * 256)

    def split(a):
        hi = a.astype(ml_dtypes.bfloat16)
        return hi, (a - hi.astype(np.float64)).astype(ml_dtypes.bfloat16)

    def left(a):
        hi, lo = split(a)
        return np.concatenate([hi, lo, hi], axis=1)

    def right(a):
        hi, lo = split(a)
        return np.concatenate([hi, lo, hi], axis=0)

    def down(n):
        ang = np.outer(alpha, np.arange(n))
        return np.concatenate([np.cos(ang), np.sin(ang)], axis=0)

    def across(pos):
        ang = np.outer(pos, beta)
        return np.concatenate([np.cos(ang), np.sin(ang)], axis=1)

    patch = np.concatenate([np.arange(64), np.arange(192, 256), np.arange(64, 192)])
    return dict(
        ky=np.concatenate(split(down(128)), axis=1),
        kx=right(across(np.arange(128))),
        fy=left(down(64).T),
        fx=np.concatenate(split(across(np.arange(128)).T * scale), axis=1),
        qy=left(down(64)),
        ex=right(across(patch)),
        ey=left(down(192)),
        gy=left(down(192).T),
        gx=right(across(patch).T * scale),
    )

NAMES = ("ky", "kx", "fy", "fx", "qy", "ex", "ey", "gy", "gx")

def hilo(a):
    hi = a.astype(BF)
    return hi, (a - hi.astype(jnp.float32)).astype(BF)

def dot(a, b):
    return jnp.dot(a, b, preferred_element_type=jnp.float32)

def rows3(a):
    hi, lo = hilo(a)
    return jnp.concatenate([hi, hi, lo], axis=0)

def cols3(a):
    hi, lo = hilo(a)
    return jnp.concatenate([hi, hi, lo], axis=1)

def pairs(z):
    cc, cs, sc, ss = z[:96, :128], z[:96, 128:], z[96:, :128], z[96:, 128:]
    re = jnp.concatenate([cc - ss, cc + ss], axis=1)
    im = jnp.concatenate([sc + cs, sc - cs], axis=1)
    return re, im

def unpair(re, im):
    p, r, q, s = re[:, :128], re[:, 128:], im[:, :128], im[:, 128:]
    top = jnp.concatenate([p + r, s - q], axis=1)
    low = jnp.concatenate([-(q + s), r - p], axis=1)
    return jnp.concatenate([top, low], axis=0)

def mask_spectrum(patch, t, e2):
    packed = dot(cols3(patch), t["ex"][...])
    re, im = pairs(dot(t["ey"][...], rows3(packed)))
    e2[:96] = re
    e2[96:] = -im

def kernel_spectrum(first, second, t, k2, p):
    wide = jnp.concatenate([first, second], axis=1)
    half = dot(t["ky"][...], jnp.concatenate([wide, wide], axis=0))
    tall = jnp.concatenate([half[:, :128], half[:, 128:]], axis=0)
    z = dot(cols3(tall), t["kx"][...])
    for i in range(2):
        re, im = pairs(z[192 * i:192 * i + 192])
        k2[p, i, :96] = re
        k2[p, i, 96:] = im

def field(t, e2, k2, f, p):
    er, ei = e2[:96], e2[96:]
    out = []
    for i in range(2):
        kr, ki = k2[p, i, :96], k2[p, i, 96:]
        out.append(dot(t["fy"][...], rows3(unpair(er * kr - ei * ki, er * ki + ei * kr))))
    hi, lo = hilo(jnp.concatenate(out, axis=0))
    first = dot(hi, t["fx"][...])
    res = first[:, :128] + first[:, 128:] + dot(lo, t["fx"][:, :128])
    f[p] = res
    return res

def spread(t, k2, q, p, tot):
    packed = dot(cols3(q), t["kx"][...])
    tr, ti = tot[:96], tot[96:]
    for i in range(2):
        qr, qi = pairs(dot(t["qy"][...], rows3(packed[64 * i:64 * i + 64])))
        kr, ki = k2[p, i, :96], k2[p, i, 96:]
        tr = tr + (qr * kr - qi * ki)
        ti = ti - (qi * kr + qr * ki)
    tot[:96] = tr
    tot[96:] = ti

def back(t, tot):
    y = dot(t["gy"][...], rows3(unpair(tot[:96], tot[96:])))
    return dot(cols3(y), t["gx"][...])

def pack(a):
    low = lax.broadcasted_iota(jnp.int32, (32, 128), 1) < 64
    top, bot = a[:32], a[32:]
    return jnp.where(low, top, pltpu.roll(bot, 64, 1)), jnp.where(low, pltpu.roll(top, 64, 1), bot)

def unpack(a, b):
    low = lax.broadcasted_iota(jnp.int32, (32, 128), 1) < 64
    return jnp.concatenate([jnp.where(low, a, pltpu.roll(b, 64, 1)), jnp.where(low, pltpu.roll(a, 64, 1), b)], axis=0)

def kernel(*refs):
    (mask_in, target_in, sets, wts, zones, counts, zone_to_set) = refs[:7]
    hbm = dict(zip(NAMES, refs[7:7 + len(NAMES)]))
    n = 7 + len(NAMES)
    resist_out, grad_out = refs[n:n + 2]
    t = dict(zip(NAMES, refs[n + 2:n + 2 + len(NAMES)]))
    (mask, target, value, halves, tall, side, chunks, info, sel, taps, wall, sv, wv, e2, k2, f, tot, co,
     gfull, ghalf, gtall, gside, want,
     tab_sem, in_sem, own_sem, s_info, r_info, s_info2, r_info2, s_w, r_w, s_w2, r_w2,
     s1, r1, s2, r2, s_m, r_m, s_m2, r_m2, s_g, r_g, s_g2, r_g2) = refs[n + 2 + len(NAMES):]

    ty, tx = lax.axis_index("ty"), lax.axis_index("tx")
    x, zl = ty // 2, ty % 2
    zh, yc = tx // YC, tx % YC
    me = ty * YC + yc

    def remote(src, dst, send, recv, to):
        return pltpu.make_async_remote_copy(src, dst, send, recv, device_id=to, device_id_type=MESH)

    def done(ref, sem):
        pltpu.make_async_copy(ref, ref, sem).wait()

    copies_in = [pltpu.make_async_copy(mask_in, mask, in_sem.at[0]),
                 pltpu.make_async_copy(target_in, target, in_sem.at[1])]
    for c in copies_in:
        c.start()
    own = pltpu.make_async_copy(sets.at[me], chunks.at[tx], own_sem.at[0])
    own.start()
    tabs = [pltpu.make_async_copy(hbm[n], t[n], tab_sem.at[i]) for i, n in enumerate(NAMES)]
    for c in tabs:
        c.start()

    yc_line = [(yc + e) % YC for e in E_ORDER[:-1]]
    ty_line = [((x + dx) % XS) * 2 + (zl + dz) % 2 for dx, dz in TY_ORDER[:-1]]
    up = 2 * zl + ZH - 1

    def z_target(m):
        if m == 3:
            return x * 2 + (1 - zl), (zh + 2) % ZH
        return x * 2 + (m - 1), (zh + up) % ZH

    z_sources = [(x * 2 + 1, (zh + ZH - 1) % ZH), (x * 2, (zh + 1) % ZH), (x * 2 + (1 - zl), (zh + 2) % ZH)]
    def beside(dr, dc):
        return (ty + dr + TYS) % TYS, (tx + dc + TXS) % TXS

    bar = pltpu.get_barrier_semaphore()
    greet = [(a, b * YC + (yc + e) % YC) for a, b in z_sources for e in E_ORDER]
    greet += [(a, tx) for a in ty_line]
    greet += [(ty, zh * YC + b) for b in yc_line]
    greet += [beside(dr, dc) for dr, dc in AROUND]
    for to in greet:
        pl.semaphore_signal(bar, 1, device_id=to, device_id_type=MESH)

    lane = lax.broadcasted_iota(jnp.int32, (1, 128), 1)
    my0, my1 = zone_to_set[zones[0]], zone_to_set[zones[1]]
    count = counts[0]
    sv[...] = jnp.where(lane == 0, my0, my1)
    wv[...] = jnp.concatenate([wts[...].astype(jnp.float32), jnp.zeros((1, 120), jnp.float32)], axis=1)
    for c in copies_in:
        c.wait()
    value[...] = 1.0 / (1.0 + jnp.exp(-mask[...]))
    halves[0], halves[1] = pack(value[...])

    pl.semaphore_wait(bar, len(greet))

    for a in ty_line:
        remote(sv, info.at[yc, ty], s_info, r_info, (a, tx)).start()
    for m in (3, 2, 1):
        a, b = z_target(m)
        remote(wv, wall.at[yc, zh], s_w, r_w, (a, b * YC + yc)).start()
    for m in (3, 2, 1):
        a, b = z_target(m)
        for e in E_ORDER:
            y2 = (yc + e) % YC
            remote(sets.at[a * YC + y2], chunks.at[tx], s1, r1, (a, b * YC + y2)).start()
    for b in yc_line:
        remote(sets.at[ty * YC + b], chunks.at[tx], s1, r1, (ty, zh * YC + b)).start()
    info[yc, ty] = sv[...]
    wall[yc, zh] = wv[...]
    done(info.at[0, pl.ds(0, 7)], r_info)
    for b in yc_line:
        remote(info.at[yc], info.at[yc], s_info2, r_info2, (ty, zh * YC + b)).start()
    done(wall.at[0, pl.ds(0, 3)], r_w)
    for b in yc_line:
        remote(wall.at[yc], wall.at[yc], s_w2, r_w2, (ty, zh * YC + b)).start()
    for dr in (-1, 0, 1):
        for dc in (-1, 1):
            remote(halves.at[(dc + 1) // 2], side.at[(1 - dr) * 2 + (1 - dc) // 2], s_m, r_m, beside(dr, dc)).start()
    for dr in (-1, 1):
        remote(value, tall.at[(1 - dr) // 2], s_m2, r_m2, beside(dr, 0)).start()
    own.wait()
    done(info.at[pl.ds(0, 7)], r_info2)
    to_scalars = pltpu.make_async_copy(info, want, own_sem.at[0])
    to_scalars.start()
    to_scalars.wait()
    done(chunks.at[pl.ds(0, 31)], r1)


    def send_slot(j):
        for n, (dx, dz) in enumerate(TY_ORDER):
            ty2 = ((x + dx) % XS) * 2 + (zl + dz) % 2
            for e in E_ORDER:
                if (dx, dz, e) == (0, 0, 0):
                    continue
                y2 = (yc + e) % YC
                i = n * YC + e
                sel[j, i] = chunks[want[y2, ty2, 0, j]]
                remote(sel.at[j, i], taps.at[j, me], s2.at[j], r2.at[j], (ty2, zh * YC + y2)).start()
        sel[j, 56] = chunks[(my0, my1)[j]]
        pltpu.make_async_copy(sel.at[j, 56], taps.at[j, me], r2.at[j]).start()

    send_slot(0)
    done(sel.at[0, pl.ds(0, 63)], s2.at[0])
    send_slot(1)

    for c in tabs:
        c.wait()
    done(side, r_m)
    done(tall, r_m2)

    def inside(dr, dc):
        row, col = ty + dr, tx + dc
        return (row >= 0) & (row < TYS) & (col >= 0) & (col < TXS)

    def gather(sides, talls, own_rows):
        blocks = []
        for dr in (-1, 0, 1):
            a, b = [jnp.where(inside(dr, dc), sides[(dr + 1) * 2 + (dc + 1) // 2], 0.0) for dc in (-1, 1)]
            mid = own_rows if dr == 0 else jnp.where(inside(dr, 0), talls[(dr + 1) // 2], 0.0)
            blocks.append((unpack(a, b), mid))
        return blocks

    blocks = gather(side, tall, value[...])
    mask_spectrum(jnp.concatenate([jnp.concatenate(b, axis=1) for b in blocks], axis=0), t, e2)
    done(info.at[0, pl.ds(0, 7)], s_info)
    done(wall.at[0, pl.ds(0, 3)], s_w)
    done(wall.at[pl.ds(0, 7)], r_w2)
    done(wall.at[pl.ds(0, 7)], s_w2)
    done(info.at[pl.ds(0, 7)], s_info2)
    done(side, s_m)
    done(tall, s_m2)
    done(chunks.at[pl.ds(0, 31)], s1)

    inverse = 1.0 / count.astype(jnp.float32)
    for j, s in enumerate((my0, my1)):
        row = wall[s % YC, s // YC]
        row = row * jnp.where(j < count, inverse, 0.0)
        for k in range(8):
            co[j * 8 + k] = jnp.broadcast_to(row[:, k:k + 1], (64, 128))

    aerial = jnp.zeros((64, 128), jnp.float32)
    for j in range(2):
        done(taps.at[j], r2.at[j])

        def spectra(k, carry):
            first, second = [taps[j, pl.ds(8 * k + 4 * i, 4)].reshape(128, 128) for i in range(2)]
            kernel_spectrum(first, second, t, k2, j * 8 + k)
            return carry

        def fields(k, total):
            p = j * 8 + k
            fp = field(t, e2, k2, f, p)
            return total + co[p] * (fp[:64] * fp[:64] + fp[64:] * fp[64:])

        lax.fori_loop(0, 8, spectra, 0, unroll=8)
        aerial = lax.fori_loop(0, 8, fields, aerial, unroll=8)

    done(sel.at[1, pl.ds(0, 63)], s2.at[1])
    resist = 1.0 / (1.0 + jnp.exp(-8.0 * (aerial - 1.0)))
    resist_out[...] = resist
    slope = 2.0 * (16.0 * (resist - target[...]) * 8.0 * resist * (1.0 - resist))
    tot[...] = jnp.zeros(tot.shape, jnp.float32)

    def three(p, carry):
        g = slope * co[p]
        spread(t, k2, jnp.concatenate([g, g], axis=0) * f[p], p, tot)
        return carry

    lax.fori_loop(0, 16, three, 0, unroll=8)
    g = back(t, tot)
    for dr in (-1, 1):
        gfull[(dr + 1) // 2] = g[(dr + 1) * 64:(dr + 2) * 64, 128:]
        remote(gfull.at[(dr + 1) // 2], gtall.at[(1 - dr) // 2], s_g2, r_g2, beside(dr, 0)).start()
    for dr in (-1, 0, 1):
        i = (dr + 1) * 2
        ghalf[i], ghalf[i + 1] = pack(g[(dr + 1) * 64:(dr + 2) * 64, :128])
        for dc in (-1, 1):
            remote(ghalf.at[i + (dc + 1) // 2], gside.at[(1 - dr) * 2 + (1 - dc) // 2], s_g, r_g, beside(dr, dc)).start()
    done(gtall, r_g2)
    done(gside, r_g)
    total = g[64:128, 128:]
    for from_sides, mid in gather(gside, gtall, 0.0):
        total = total + from_sides + mid
    m = value[...]
    grad_out[...] = total * m * (1.0 - m)
    done(gtall, s_g2)
    done(gside, s_g)


def body(mask_param, target, kernel_sets, kernel_weights, tile_zones, tile_counts, zone_to_set):
    tb = tables()
    f32, i32, dma = jnp.float32, jnp.int32, pltpu.SemaphoreType.DMA
    any_, vmem = pl.BlockSpec(memory_space=pltpu.HBM), pl.BlockSpec(memory_space=pltpu.VMEM)
    smem = pl.BlockSpec(memory_space=pltpu.SMEM)
    scratch = [pltpu.VMEM(tb[n].shape, BF) for n in NAMES]
    scratch += [
        pltpu.VMEM((64, 128), f32), pltpu.VMEM((64, 128), f32), pltpu.VMEM((64, 128), f32),
        pltpu.VMEM((2, 32, 128), f32), pltpu.VMEM((2, 64, 128), f32), pltpu.VMEM((6, 32, 128), f32),
        pltpu.VMEM((32, 32, 128), BF), pltpu.VMEM((YC, TYS, 1, 128), i32),
        pltpu.VMEM((2, 64, 32, 128), BF), pltpu.VMEM((2, 64, 32, 128), BF),
        pltpu.VMEM((YC, ZH, 1, 128), f32), pltpu.VMEM((1, 128), i32), pltpu.VMEM((1, 128), f32),
        pltpu.VMEM((192, 256), f32), pltpu.VMEM((16, 2, 192, 256), f32), pltpu.VMEM((16, 128, 128), f32),
        pltpu.VMEM((192, 256), f32), pltpu.VMEM((16, 64, 128), f32),
        pltpu.VMEM((2, 64, 128), f32), pltpu.VMEM((6, 32, 128), f32),
        pltpu.VMEM((2, 64, 128), f32), pltpu.VMEM((6, 32, 128), f32),
        pltpu.SMEM((YC, TYS, 1, 128), i32),
        dma((len(NAMES),)), dma((2,)), dma((1,)),
        dma, dma, dma, dma, dma, dma, dma, dma,
        dma, dma, dma((2,)), dma((2,)), dma, dma, dma, dma, dma, dma, dma, dma,
    ]
    return pl.pallas_call(
        kernel,
        out_shape=(jax.ShapeDtypeStruct((64, 128), f32), jax.ShapeDtypeStruct((64, 128), f32)),
        in_specs=[any_, any_, any_, vmem, smem, smem, smem] + [any_] * len(NAMES),
        out_specs=(vmem, vmem),
        scratch_shapes=scratch,
        compiler_params=pltpu.CompilerParams(
            collective_id=1, has_side_effects=True, vmem_limit_bytes=63 << 20
        ),
        name="litho",
    )(
        mask_param, target, kernel_sets.reshape(64, 32, 128), kernel_weights,
        tile_zones.reshape(2), tile_counts.reshape(1), zone_to_set,
        *[jnp.asarray(tb[n]) for n in NAMES],
    )


def solution(mesh):
    in_specs = (
        P("ty", "tx"), P("ty", "tx"), P("tx", None, None, None, None), P("tx", None),
        P("ty", "tx", None), P("ty", "tx"), P(),
    )
    return jax.shard_map(
        body, mesh=mesh, in_specs=in_specs, out_specs=(P("ty", "tx"), P("ty", "tx")), check_vma=False
    )
```

time: 63.9 us -> 54.8 us (0.86)
  Pallas kernels: 60.5 us -> 51.3 us
    pallas_call x1, Pallas kernels: 60.5 us -> 51.3 us  [body(): pl.pallas_call(kernel, out_shape=(jax.ShapeDtypeStruct((64, 128), f32), j...]
where the time goes in v2:
time: 54.8 us; the launch traced here: 54.6 us
  Pallas kernels  51.3 us (94%)
  local copies, waits for them, and re-layouts  2 us (4%)
  between operations  1.29 us (2%)
    pallas_call x1, Pallas kernels, body(): pl.pallas_call(kernel, out_shape=(jax.ShapeDtypeStruct((64, 128), f32), j...  51.3 us
    unnamed x4, local copies, waits for them, and re-layouts  2 us

profile of v2, /device:TPU:32, one launch (start us, length us, event | category | flops | bytes accessed | tf_op | source)
XLA Modules:
  0.0 54.6 jit_solution(925300777486444324)
XLA Ops:
  1.3 51.3 %litho.1 = (f32[64,128]{1,0:T(8,128)}, f32[64,128]{1,0:T(8,128)}) custom-call(f32[64,128]{1,0:T(8,128)} %refs_0_.1, f32[64,128]{1,0:T(8,128)} %refs_1_.1, bf16[64,32,128]{2,1,0:T(8,128)(2,1)} %bitcast.4, bf16[1,8]{1,0:T(2,128)(2,1)} %refs_3_.1, s32[2]{0:T(128)} %bitcast.5, s32[1]{0:T(128)} %bitcast.3.refs_5_, s32[32]{0:T(128)} %refs_6_.1, ...), custom_call_target="tpu_custom_call" | custom-call | tf_op jit(solution)/shard_map/litho/pallas_call | solution.py:362
  52.6 0.0 copy-start
  52.6 1.4 %copy.21 = f32[64,128]{1,0:T(8,128)} copy(f32[64,128]{1,0:T(8,128)} %get-tuple-element.4) | data formatting | bytes 65536
  54.0 0.0 copy-done
  54.0 0.6 %copy.22 = f32[64,128]{1,0:T(8,128)} copy(f32[64,128]{1,0:T(8,128)S(1)} %copy-done) | data formatting | bytes 65536
Async XLA Ops:
  52.6 1.4 %copy-start = (f32[64,128]{1,0:T(8,128)S(1)}, f32[64,128]{1,0:T(8,128)}, u32[]{:S(2)}) copy-start(f32[64,128]{1,0:T(8,128)} %get-tuple-element.5) | copy-start | bytes 98308

commit v3 on v2

--- a/solution.py
+++ b/solution.py
@@ -10,9 +10,9 @@
 from jax.sharding import PartitionSpec as P
 
 BF = jnp.bfloat16
+GROUP = 4
 MESH = pl.DeviceIdType.MESH
 XS, YC, ZH = 4, 8, 4
-MEMBERS = XS * YC
 TYS, TXS = 8, 32
 AROUND = [(dr, dc) for dr in (-1, 0, 1) for dc in (-1, 0, 1) if (dr, dc) != (0, 0)]
 E_ORDER = (4, 3, 5, 2, 6, 1, 7, 0)
@@ -93,38 +93,42 @@
     e2[:96] = re
     e2[96:] = -im
 
-def kernel_spectrum(first, second, t, k2, p):
-    wide = jnp.concatenate([first, second], axis=1)
+def kernel_spectra(taps, t, k2, ps):
+    wide = jnp.concatenate([c for pair in taps for c in pair], axis=1)
     half = dot(t["ky"][...], jnp.concatenate([wide, wide], axis=0))
-    tall = jnp.concatenate([half[:, :128], half[:, 128:]], axis=0)
+    n = 2 * len(ps)
+    tall = jnp.concatenate([half[:, 128 * i:128 * i + 128] for i in range(n)], axis=0)
     z = dot(cols3(tall), t["kx"][...])
-    for i in range(2):
+    for i in range(n):
         re, im = pairs(z[192 * i:192 * i + 192])
-        k2[p, i, :96] = re
-        k2[p, i, 96:] = im
-
-def field(t, e2, k2, f, p):
+        k2[ps[i // 2], i % 2, :96] = re
+        k2[ps[i // 2], i % 2, 96:] = im
+
+
+def fields_of(t, e2, k2, f, ps):
     er, ei = e2[:96], e2[96:]
-    out = []
-    for i in range(2):
-        kr, ki = k2[p, i, :96], k2[p, i, 96:]
-        out.append(dot(t["fy"][...], rows3(unpair(er * kr - ei * ki, er * ki + ei * kr))))
-    hi, lo = hilo(jnp.concatenate(out, axis=0))
+    n = 2 * len(ps)
+    parts = []
+    for i in range(n):
+        kr, ki = k2[ps[i // 2], i % 2, :96], k2[ps[i // 2], i % 2, 96:]
+        parts.append(rows3(unpair(er * kr - ei * ki, er * ki + ei * kr)))
+    y = dot(t["fy"][...], jnp.concatenate(parts, axis=1))
+    hi, lo = hilo(jnp.concatenate([y[:, 256 * i:256 * i + 256] for i in range(n)], axis=0))
     first = dot(hi, t["fx"][...])
     res = first[:, :128] + first[:, 128:] + dot(lo, t["fx"][:, :128])
-    f[p] = res
-    return res
-
-def spread(t, k2, q, p, tot):
-    packed = dot(cols3(q), t["kx"][...])
-    tr, ti = tot[:96], tot[96:]
-    for i in range(2):
+    for i, p in enumerate(ps):
+        f[p] = res[128 * i:128 * i + 128]
+    return [res[128 * i:128 * i + 128] for i in range(len(ps))]
+
+
+def spread(t, k2, qs, ps, tot):
+    packed = dot(cols3(jnp.concatenate(qs, axis=0)), t["kx"][...])
+    for i in range(2 * len(ps)):
         qr, qi = pairs(dot(t["qy"][...], rows3(packed[64 * i:64 * i + 64])))
-        kr, ki = k2[p, i, :96], k2[p, i, 96:]
-        tr = tr + (qr * kr - qi * ki)
-        ti = ti - (qi * kr + qr * ki)
-    tot[:96] = tr
-    tot[96:] = ti
+        kr, ki = k2[ps[i // 2], i % 2, :96], k2[ps[i // 2], i % 2, 96:]
+        tot[:96] += qr * kr - qi * ki
+        tot[96:] -= qi * kr + qr * ki
+
 
 def back(t, tot):
     y = dot(t["gy"][...], rows3(unpair(tot[:96], tot[96:])))
@@ -143,12 +147,12 @@
     (mask_in, target_in, sets, wts, zones, counts, zone_to_set) = refs[:7]
     hbm = dict(zip(NAMES, refs[7:7 + len(NAMES)]))
     n = 7 + len(NAMES)
-    resist_out, grad_out = refs[n:n + 2]
-    t = dict(zip(NAMES, refs[n + 2:n + 2 + len(NAMES)]))
+    out = refs[n]
+    t = dict(zip(NAMES, refs[n + 1:n + 1 + len(NAMES)]))
     (mask, target, value, halves, tall, side, chunks, info, sel, taps, wall, sv, wv, e2, k2, f, tot, co,
      gfull, ghalf, gtall, gside, want,
      tab_sem, in_sem, own_sem, s_info, r_info, s_info2, r_info2, s_w, r_w, s_w2, r_w2,
-     s1, r1, s2, r2, s_m, r_m, s_m2, r_m2, s_g, r_g, s_g2, r_g2) = refs[n + 2 + len(NAMES):]
+     s1, r1, s2, r2, s_m, r_m, s_m2, r_m2, s_g, r_g, s_g2, r_g2) = refs[n + 1 + len(NAMES):]
 
     ty, tx = lax.axis_index("ty"), lax.axis_index("tx")
     x, zl = ty // 2, ty % 2
@@ -160,6 +164,27 @@
 
     def done(ref, sem):
         pltpu.make_async_copy(ref, ref, sem).wait()
+
+    yc_line = [(yc + e) % YC for e in E_ORDER[:-1]]
+    ty_line = [((x + dx) % XS) * 2 + (zl + dz) % 2 for dx, dz in TY_ORDER[:-1]]
+    up = 2 * zl + ZH - 1
+
+    def z_target(m):
+        if m == 3:
+            return x * 2 + (1 - zl), (zh + 2) % ZH
+        return x * 2 + (m - 1), (zh + up) % ZH
+
+    z_sources = [(x * 2 + 1, (zh + ZH - 1) % ZH), (x * 2, (zh + 1) % ZH), (x * 2 + (1 - zl), (zh + 2) % ZH)]
+    def beside(dr, dc):
+        return (ty + dr + TYS) % TYS, (tx + dc + TXS) % TXS
+
+    bar = pltpu.get_barrier_semaphore()
+    greet = [(a, b * YC + (yc + e) % YC) for a, b in z_sources for e in E_ORDER]
+    greet += [(a, tx) for a in ty_line]
+    greet += [(ty, zh * YC + b) for b in yc_line]
+    greet += [beside(dr, dc) for dr, dc in AROUND if dc != 0]
+    for to in greet:
+        pl.semaphore_signal(bar, 1, device_id=to, device_id_type=MESH)
 
     copies_in = [pltpu.make_async_copy(mask_in, mask, in_sem.at[0]),
                  pltpu.make_async_copy(target_in, target, in_sem.at[1])]
@@ -170,27 +195,6 @@
     tabs = [pltpu.make_async_copy(hbm[n], t[n], tab_sem.at[i]) for i, n in enumerate(NAMES)]
     for c in tabs:
         c.start()
-
-    yc_line = [(yc + e) % YC for e in E_ORDER[:-1]]
-    ty_line = [((x + dx) % XS) * 2 + (zl + dz) % 2 for dx, dz in TY_ORDER[:-1]]
-    up = 2 * zl + ZH - 1
-
-    def z_target(m):
-        if m == 3:
-            return x * 2 + (1 - zl), (zh + 2) % ZH
-        return x * 2 + (m - 1), (zh + up) % ZH
-
-    z_sources = [(x * 2 + 1, (zh + ZH - 1) % ZH), (x * 2, (zh + 1) % ZH), (x * 2 + (1 - zl), (zh + 2) % ZH)]
-    def beside(dr, dc):
-        return (ty + dr + TYS) % TYS, (tx + dc + TXS) % TXS
-
-    bar = pltpu.get_barrier_semaphore()
-    greet = [(a, b * YC + (yc + e) % YC) for a, b in z_sources for e in E_ORDER]
-    greet += [(a, tx) for a in ty_line]
-    greet += [(ty, zh * YC + b) for b in yc_line]
-    greet += [beside(dr, dc) for dr, dc in AROUND]
-    for to in greet:
-        pl.semaphore_signal(bar, 1, device_id=to, device_id_type=MESH)
 
     lane = lax.broadcasted_iota(jnp.int32, (1, 128), 1)
     my0, my1 = zone_to_set[zones[0]], zone_to_set[zones[1]]
@@ -293,31 +297,29 @@
     for j in range(2):
         done(taps.at[j], r2.at[j])
 
-        def spectra(k, carry):
-            first, second = [taps[j, pl.ds(8 * k + 4 * i, 4)].reshape(128, 128) for i in range(2)]
-            kernel_spectrum(first, second, t, k2, j * 8 + k)
-            return carry
-
-        def fields(k, total):
-            p = j * 8 + k
-            fp = field(t, e2, k2, f, p)
-            return total + co[p] * (fp[:64] * fp[:64] + fp[64:] * fp[64:])
-
-        lax.fori_loop(0, 8, spectra, 0, unroll=8)
-        aerial = lax.fori_loop(0, 8, fields, aerial, unroll=8)
+        for h in range(0, 8, GROUP):
+            chosen = [
+                tuple(taps[j, 8 * k + 4 * i:8 * k + 4 * i + 4].reshape(128, 128) for i in range(2))
+                for k in range(h, h + GROUP)
+            ]
+            kernel_spectra(chosen, t, k2, range(j * 8 + h, j * 8 + h + GROUP))
+        for h in range(0, 8, GROUP):
+            ps = range(j * 8 + h, j * 8 + h + GROUP)
+            for p, fp in zip(ps, fields_of(t, e2, k2, f, ps)):
+                aerial = aerial + co[p] * (fp[:64] * fp[:64] + fp[64:] * fp[64:])
 
     done(sel.at[1, pl.ds(0, 63)], s2.at[1])
     resist = 1.0 / (1.0 + jnp.exp(-8.0 * (aerial - 1.0)))
-    resist_out[...] = resist
+    out[0] = resist
     slope = 2.0 * (16.0 * (resist - target[...]) * 8.0 * resist * (1.0 - resist))
     tot[...] = jnp.zeros(tot.shape, jnp.float32)
 
-    def three(p, carry):
-        g = slope * co[p]
-        spread(t, k2, jnp.concatenate([g, g], axis=0) * f[p], p, tot)
+    def some(h, carry):
+        ps = [GROUP * h + i for i in range(GROUP)]
+        spread(t, k2, [jnp.concatenate([slope * co[p]] * 2, axis=0) * f[p] for p in ps], ps, tot)
         return carry
 
-    lax.fori_loop(0, 16, three, 0, unroll=8)
+    lax.fori_loop(0, 16 // GROUP, some, 0, unroll=2)
     g = back(t, tot)
     for dr in (-1, 1):
         gfull[(dr + 1) // 2] = g[(dr + 1) * 64:(dr + 2) * 64, 128:]
@@ -333,7 +335,7 @@
     for from_sides, mid in gather(gside, gtall, 0.0):
         total = total + from_sides + mid
     m = value[...]
-    grad_out[...] = total * m * (1.0 - m)
+    out[1] = total * m * (1.0 - m)
     done(gtall, s_g2)
     done(gside, s_g)
 
@@ -359,11 +361,11 @@
         dma, dma, dma, dma, dma, dma, dma, dma,
         dma, dma, dma((2,)), dma((2,)), dma, dma, dma, dma, dma, dma, dma, dma,
     ]
-    return pl.pallas_call(
+    out = pl.pallas_call(
         kernel,
-        out_shape=(jax.ShapeDtypeStruct((64, 128), f32), jax.ShapeDtypeStruct((64, 128), f32)),
+        out_shape=jax.ShapeDtypeStruct((2, 64, 128), f32),
         in_specs=[any_, any_, any_, vmem, smem, smem, smem] + [any_] * len(NAMES),
-        out_specs=(vmem, vmem),
+        out_specs=vmem,
         scratch_shapes=scratch,
         compiler_params=pltpu.CompilerParams(
             collective_id=1, has_side_effects=True, vmem_limit_bytes=63 << 20
@@ -374,6 +376,7 @@
         tile_zones.reshape(2), tile_counts.reshape(1), zone_to_set,
         *[jnp.asarray(tb[n]) for n in NAMES],
     )
+    return out[0], out[1]
 
 
 def solution(mesh):

time: 54.8 us -> 51.9 us (0.947)
  Pallas kernels: 51.3 us -> 48.8 us
  local copies, waits for them, and re-layouts: 2 us -> 1.4 us
    pallas_call x1, Pallas kernels: 51.3 us -> 48.8 us  [body(): pl.pallas_call(kernel, out_shape=jax.ShapeDtypeStruct((2, 64, 128), f32),...]
    unnamed x4 -> x0, local copies, waits for them, and re-layouts: 2 us -> none
    squeeze x0 -> x1, local copies, waits for them, and re-layouts: none -> 1.4 us  [body(): return (out[0], out[1])]
where the time goes in v3:
time: 51.9 us; the launch traced here: 51.5 us
  Pallas kernels  48.8 us (94%)
  local copies, waits for them, and re-layouts  1.4 us (3%)
  between operations  1.29 us (2%)
    pallas_call x1, Pallas kernels, body(): pl.pallas_call(kernel, out_shape=jax.ShapeDtypeStruct((2, 64, 128), f32),...  48.8 us
    squeeze x1, local copies, waits for them, and re-layouts, body(): return (out[0], out[1])  1.4 us

profile of v3, /device:TPU:32, one launch (start us, length us, event | category | flops | bytes accessed | tf_op | source)
XLA Modules:
  0.0 51.5 jit_solution(15511280379643052907)
XLA Ops:
  1.3 48.8 %litho.1 = f32[2,64,128]{2,1,0:T(8,128)} custom-call(f32[64,128]{1,0:T(8,128)} %refs_0_.1, f32[64,128]{1,0:T(8,128)} %refs_1_.1, bf16[64,32,128]{2,1,0:T(8,128)(2,1)} %bitcast.8, bf16[1,8]{1,0:T(2,128)(2,1)} %refs_3_.1, s32[2]{0:T(128)} %bitcast.9, s32[1]{0:T(128)} %bitcast.7.refs_5_, s32[32]{0:T(128)} %refs_6_.1, bf16[192,256]{1,0:T(8,128)(2,1)} %constant.18.clone.refs_7_, ...), custom_call_target="tpu_custom_call" | custom-call | tf_op jit(solution)/shard_map/litho/pallas_call | solution.py:364
  50.1 1.4 %slice_bitcast_fusion = (f32[64,128]{1,0:T(8,128)}, f32[64,128]{1,0:T(8,128)}) fusion(f32[2,64,128]{2,1,0:T(8,128)} %litho.1), kind=kLoop, calls=%fused_computation | loop fusion | bytes 131072 | tf_op jit(solution)/shard_map/squeeze | solution.py:379

commit v4 on v3

--- a/solution.py
+++ b/solution.py
@@ -149,7 +149,7 @@
     n = 7 + len(NAMES)
     out = refs[n]
     t = dict(zip(NAMES, refs[n + 1:n + 1 + len(NAMES)]))
-    (mask, target, value, halves, tall, side, chunks, info, sel, taps, wall, sv, wv, e2, k2, f, tot, co,
+    (mask, target, value, halves, tall, side, chunks, column, info, sel, taps, wall, sv, wv, e2, k2, f, tot, co,
      gfull, ghalf, gtall, gside, want,
      tab_sem, in_sem, own_sem, s_info, r_info, s_info2, r_info2, s_w, r_w, s_w2, r_w2,
      s1, r1, s2, r2, s_m, r_m, s_m2, r_m2, s_g, r_g, s_g2, r_g2) = refs[n + 1 + len(NAMES):]
@@ -199,7 +199,7 @@
     lane = lax.broadcasted_iota(jnp.int32, (1, 128), 1)
     my0, my1 = zone_to_set[zones[0]], zone_to_set[zones[1]]
     count = counts[0]
-    sv[...] = jnp.where(lane == 0, my0, my1)
+    sv[...] = jnp.where(lane % 2 == 0, my0, my1)
     wv[...] = jnp.concatenate([wts[...].astype(jnp.float32), jnp.zeros((1, 120), jnp.float32)], axis=1)
     for c in copies_in:
         c.wait()
@@ -209,7 +209,7 @@
     pl.semaphore_wait(bar, len(greet))
 
     for a in ty_line:
-        remote(sv, info.at[yc, ty], s_info, r_info, (a, tx)).start()
+        remote(sv, column.at[ty], s_info, r_info, (a, tx)).start()
     for m in (3, 2, 1):
         a, b = z_target(m)
         remote(wv, wall.at[yc, zh], s_w, r_w, (a, b * YC + yc)).start()
@@ -220,9 +220,13 @@
             remote(sets.at[a * YC + y2], chunks.at[tx], s1, r1, (a, b * YC + y2)).start()
     for b in yc_line:
         remote(sets.at[ty * YC + b], chunks.at[tx], s1, r1, (ty, zh * YC + b)).start()
-    info[yc, ty] = sv[...]
+    column[ty] = sv[...]
     wall[yc, zh] = wv[...]
-    done(info.at[0, pl.ds(0, 7)], r_info)
+    done(column.at[pl.ds(0, 7)], r_info)
+    merged = column[0]
+    for i in range(1, TYS):
+        merged = jnp.where(lane // 2 == i, column[i], merged)
+    info[yc] = merged
     for b in yc_line:
         remote(info.at[yc], info.at[yc], s_info2, r_info2, (ty, zh * YC + b)).start()
     done(wall.at[0, pl.ds(0, 3)], r_w)
@@ -249,13 +253,12 @@
                     continue
                 y2 = (yc + e) % YC
                 i = n * YC + e
-                sel[j, i] = chunks[want[y2, ty2, 0, j]]
+                sel[j, i] = chunks[want[y2, 0, 2 * ty2 + j]]
                 remote(sel.at[j, i], taps.at[j, me], s2.at[j], r2.at[j], (ty2, zh * YC + y2)).start()
         sel[j, 56] = chunks[(my0, my1)[j]]
         pltpu.make_async_copy(sel.at[j, 56], taps.at[j, me], r2.at[j]).start()
 
     send_slot(0)
-    done(sel.at[0, pl.ds(0, 63)], s2.at[0])
     send_slot(1)
 
     for c in tabs:
@@ -277,7 +280,7 @@
 
     blocks = gather(side, tall, value[...])
     mask_spectrum(jnp.concatenate([jnp.concatenate(b, axis=1) for b in blocks], axis=0), t, e2)
-    done(info.at[0, pl.ds(0, 7)], s_info)
+    done(column.at[pl.ds(0, 7)], s_info)
     done(wall.at[0, pl.ds(0, 3)], s_w)
     done(wall.at[pl.ds(0, 7)], r_w2)
     done(wall.at[pl.ds(0, 7)], s_w2)
@@ -308,7 +311,6 @@
             for p, fp in zip(ps, fields_of(t, e2, k2, f, ps)):
                 aerial = aerial + co[p] * (fp[:64] * fp[:64] + fp[64:] * fp[64:])
 
-    done(sel.at[1, pl.ds(0, 63)], s2.at[1])
     resist = 1.0 / (1.0 + jnp.exp(-8.0 * (aerial - 1.0)))
     out[0] = resist
     slope = 2.0 * (16.0 * (resist - target[...]) * 8.0 * resist * (1.0 - resist))
@@ -321,14 +323,14 @@
 
     lax.fori_loop(0, 16 // GROUP, some, 0, unroll=2)
     g = back(t, tot)
-    for dr in (-1, 1):
-        gfull[(dr + 1) // 2] = g[(dr + 1) * 64:(dr + 2) * 64, 128:]
-        remote(gfull.at[(dr + 1) // 2], gtall.at[(1 - dr) // 2], s_g2, r_g2, beside(dr, 0)).start()
-    for dr in (-1, 0, 1):
+    for dr in (-1, 1, 0):
         i = (dr + 1) * 2
         ghalf[i], ghalf[i + 1] = pack(g[(dr + 1) * 64:(dr + 2) * 64, :128])
         for dc in (-1, 1):
             remote(ghalf.at[i + (dc + 1) // 2], gside.at[(1 - dr) * 2 + (1 - dc) // 2], s_g, r_g, beside(dr, dc)).start()
+        if dr != 0:
+            gfull[(dr + 1) // 2] = g[(dr + 1) * 64:(dr + 2) * 64, 128:]
+            remote(gfull.at[(dr + 1) // 2], gtall.at[(1 - dr) // 2], s_g2, r_g2, beside(dr, 0)).start()
     done(gtall, r_g2)
     done(gside, r_g)
     total = g[64:128, 128:]
@@ -336,6 +338,8 @@
         total = total + from_sides + mid
     m = value[...]
     out[1] = total * m * (1.0 - m)
+    done(sel.at[0, pl.ds(0, 63)], s2.at[0])
+    done(sel.at[1, pl.ds(0, 63)], s2.at[1])
     done(gtall, s_g2)
     done(gside, s_g)
 
@@ -349,14 +353,14 @@
     scratch += [
         pltpu.VMEM((64, 128), f32), pltpu.VMEM((64, 128), f32), pltpu.VMEM((64, 128), f32),
         pltpu.VMEM((2, 32, 128), f32), pltpu.VMEM((2, 64, 128), f32), pltpu.VMEM((6, 32, 128), f32),
-        pltpu.VMEM((32, 32, 128), BF), pltpu.VMEM((YC, TYS, 1, 128), i32),
+        pltpu.VMEM((32, 32, 128), BF), pltpu.VMEM((TYS, 1, 128), i32), pltpu.VMEM((YC, 1, 128), i32),
         pltpu.VMEM((2, 64, 32, 128), BF), pltpu.VMEM((2, 64, 32, 128), BF),
         pltpu.VMEM((YC, ZH, 1, 128), f32), pltpu.VMEM((1, 128), i32), pltpu.VMEM((1, 128), f32),
         pltpu.VMEM((192, 256), f32), pltpu.VMEM((16, 2, 192, 256), f32), pltpu.VMEM((16, 128, 128), f32),
         pltpu.VMEM((192, 256), f32), pltpu.VMEM((16, 64, 128), f32),
         pltpu.VMEM((2, 64, 128), f32), pltpu.VMEM((6, 32, 128), f32),
         pltpu.VMEM((2, 64, 128), f32), pltpu.VMEM((6, 32, 128), f32),
-        pltpu.SMEM((YC, TYS, 1, 128), i32),
+        pltpu.SMEM((YC, 1, 128), i32),
         dma((len(NAMES),)), dma((2,)), dma((1,)),
         dma, dma, dma, dma, dma, dma, dma, dma,
         dma, dma, dma((2,)), dma((2,)), dma, dma, dma, dma, dma, dma, dma, dma,

time: 51.9 us -> 50.7 us (0.977)
  Pallas kernels: 48.8 us -> 47.5 us
    pallas_call x1, Pallas kernels: 48.8 us -> 47.5 us  [body(): pl.pallas_call(kernel, out_shape=jax.ShapeDtypeStruct((2, 64, 128), f32),...]
where the time goes in v4:
time: 50.7 us; the launch traced here: 50.2 us
  Pallas kernels  47.5 us (94%)
  local copies, waits for them, and re-layouts  1.4 us (3%)
  between operations  1.29 us (3%)
    pallas_call x1, Pallas kernels, body(): pl.pallas_call(kernel, out_shape=jax.ShapeDtypeStruct((2, 64, 128), f32),...  47.5 us
    squeeze x1, local copies, waits for them, and re-layouts, body(): return (out[0], out[1])  1.4 us

profile of v4, /device:TPU:32, one launch (start us, length us, event | category | flops | bytes accessed | tf_op | source)
XLA Modules:
  0.0 50.2 jit_solution(15308121316493423989)
XLA Ops:
  1.3 47.5 %litho.1 = f32[2,64,128]{2,1,0:T(8,128)} custom-call(f32[64,128]{1,0:T(8,128)} %refs_0_.1, f32[64,128]{1,0:T(8,128)} %refs_1_.1, bf16[64,32,128]{2,1,0:T(8,128)(2,1)} %bitcast.8, bf16[1,8]{1,0:T(2,128)(2,1)} %refs_3_.1, s32[2]{0:T(128)} %bitcast.9, s32[1]{0:T(128)} %bitcast.7.refs_5_, s32[32]{0:T(128)} %refs_6_.1, bf16[192,256]{1,0:T(8,128)(2,1)} %constant.18.clone.refs_7_, ...), custom_call_target="tpu_custom_call" | custom-call | tf_op jit(solution)/shard_map/litho/pallas_call | solution.py:368
  48.8 1.4 %slice_bitcast_fusion = (f32[64,128]{1,0:T(8,128)}, f32[64,128]{1,0:T(8,128)}) fusion(f32[2,64,128]{2,1,0:T(8,128)} %litho.1), kind=kLoop, calls=%fused_computation | loop fusion | bytes 131072 | tf_op jit(solution)/shard_map/squeeze | solution.py:383

commit v5 on v4

--- a/solution.py
+++ b/solution.py
@@ -54,7 +54,7 @@
         qy=left(down(64)),
         ex=right(across(patch)),
         ey=left(down(192)),
-        gy=left(down(192).T),
+        gy=left(down(192).T[np.concatenate([np.arange(64), np.arange(128, 192), np.arange(64, 128)])]),
         gx=right(across(patch).T * scale),
     )
 
@@ -131,8 +131,9 @@
 
 
 def back(t, tot):
-    y = dot(t["gy"][...], rows3(unpair(tot[:96], tot[96:])))
-    return dot(cols3(y), t["gx"][...])
+    tall = rows3(unpair(tot[:96], tot[96:]))
+    return [dot(cols3(dot(t["gy"][a:b, :], tall)), t["gx"][...]) for a, b in ((0, 128), (128, 192))]
+
 
 def pack(a):
     low = lax.broadcasted_iota(jnp.int32, (32, 128), 1) < 64
@@ -322,18 +323,19 @@
         return carry
 
     lax.fori_loop(0, 16 // GROUP, some, 0, unroll=2)
-    g = back(t, tot)
+    outer, middle = back(t, tot)
     for dr in (-1, 1, 0):
         i = (dr + 1) * 2
-        ghalf[i], ghalf[i + 1] = pack(g[(dr + 1) * 64:(dr + 2) * 64, :128])
+        g = middle if dr == 0 else outer[(dr + 1) * 32:(dr + 1) * 32 + 64]
+        ghalf[i], ghalf[i + 1] = pack(g[:, :128])
         for dc in (-1, 1):
             remote(ghalf.at[i + (dc + 1) // 2], gside.at[(1 - dr) * 2 + (1 - dc) // 2], s_g, r_g, beside(dr, dc)).start()
         if dr != 0:
-            gfull[(dr + 1) // 2] = g[(dr + 1) * 64:(dr + 2) * 64, 128:]
+            gfull[(dr + 1) // 2] = g[:, 128:]
             remote(gfull.at[(dr + 1) // 2], gtall.at[(1 - dr) // 2], s_g2, r_g2, beside(dr, 0)).start()
     done(gtall, r_g2)
     done(gside, r_g)
-    total = g[64:128, 128:]
+    total = middle[:, 128:]
     for from_sides, mid in gather(gside, gtall, 0.0):
         total = total + from_sides + mid
     m = value[...]

time: 50.7 us -> 50.6 us (level)
  no operation moved by 1% of the time
where the time goes in v5:
time: 50.6 us; the launch traced here: 50.2 us
  Pallas kernels  47.5 us (94%)
  local copies, waits for them, and re-layouts  1.4 us (3%)
  between operations  1.29 us (3%)
    pallas_call x1, Pallas kernels, body(): pl.pallas_call(kernel, out_shape=jax.ShapeDtypeStruct((2, 64, 128), f32),...  47.5 us
    squeeze x1, local copies, waits for them, and re-layouts, body(): return (out[0], out[1])  1.4 us

profile of v5, /device:TPU:32, one launch (start us, length us, event | category | flops | bytes accessed | tf_op | source)
XLA Modules:
  0.0 50.2 jit_solution(14490767025601067735)
XLA Ops:
  1.3 47.5 %litho.1 = f32[2,64,128]{2,1,0:T(8,128)} custom-call(f32[64,128]{1,0:T(8,128)} %refs_0_.1, f32[64,128]{1,0:T(8,128)} %refs_1_.1, bf16[64,32,128]{2,1,0:T(8,128)(2,1)} %bitcast.8, bf16[1,8]{1,0:T(2,128)(2,1)} %refs_3_.1, s32[2]{0:T(128)} %bitcast.9, s32[1]{0:T(128)} %bitcast.7.refs_5_, s32[32]{0:T(128)} %refs_6_.1, bf16[192,256]{1,0:T(8,128)(2,1)} %constant.18.clone.refs_7_, ...), custom_call_target="tpu_custom_call" | custom-call | tf_op jit(solution)/shard_map/litho/pallas_call | solution.py:370
  48.7 1.4 %slice_bitcast_fusion = (f32[64,128]{1,0:T(8,128)}, f32[64,128]{1,0:T(8,128)}) fusion(f32[2,64,128]{2,1,0:T(8,128)} %litho.1), kind=kLoop, calls=%fused_computation | loop fusion | bytes 131072 | tf_op jit(solution)/shard_map/squeeze | solution.py:385
